TPU v7x, 32 devices: a whole 2x2x4 slice. The times are simulated.
32 devices in a mesh: fsdp: 8 (over z, x), dp: 4 (over y, core).
Axes of the slice: x: 2, y: 2, z: 4, core: 2. Of those that a mesh axis runs over, the one named last changes fastest.
Arguments:
- tokens: bfloat16 [16384, 768], P(('fsdp', 'dp')), may hold values from -6 to 6
- cotangent: bfloat16 [16384, 768], P(('fsdp', 'dp')), may hold values from -6 to 6
- seq_lens: int32 [32, 4], P(('fsdp', 'dp')), may hold values from 0 to 512, as said below
- routes: int32 [16384, 1], P(('fsdp', 'dp')), may hold values from 0 to 7; in each aligned block of 512 rows (0 to 511, 512 to 1023, ...) at most 128 rows name the same one
- norm_gains: bfloat16 [2, 768], P(None, ('fsdp', 'dp')), may hold values from 0.5 to 1.5
- qkv_weight: bfloat16 [768, 2304], P(('fsdp', 'dp')), may hold values from -0.21875 to 0.21875
- out_weight: bfloat16 [768, 768], P(('fsdp', 'dp')), may hold values from -0.875 to 0.875
- router_weight: bfloat16 [768, 8], P(('fsdp', 'dp')), may hold values from -0.15625 to 0.15625
- rel_bias: float32 [32, 12], replicated, may hold values from -4 to 4
- expert_in: bfloat16 [8, 768, 3072], P('dp', None, 'fsdp'), may hold values from -0.21875 to 0.21875
- expert_out: bfloat16 [8, 3072, 768], P('dp', 'fsdp'), may hold values from -0.875 to 0.875
Outputs:
- mixed: bfloat16 [16384, 768], P(('fsdp', 'dp'))
- tokens_grad: float32 [16384, 768], P(('fsdp', 'dp'))
- gains_grad: float32 [2, 768], P(None, ('fsdp', 'dp'))
- qkv_grad: float32 [768, 2304], P(('fsdp', 'dp'))
- out_grad: float32 [768, 768], P(('fsdp', 'dp'))
- router_grad: float32 [768, 8], P(('fsdp', 'dp'))
- bias_grad: float32 [32, 12], replicated
- expert_in_grad: float32 [8, 768, 3072], P('dp', None, 'fsdp')
- expert_out_grad: float32 [8, 3072, 768], P('dp', 'fsdp')
Inputs may be any that keep to these rules, and one draw needn't show every extreme that they name: `seq_lens`: row b lists the sequences of block b in order from its first slot; a row sums to 256 or more and to 512 or less; some row is one sequence of 512. `routes`: among the 512 rows of one device no expert is named more than 128 times.
All inputs are finite; a program needn't handle non-finite values.
Results may differ from a plain program's by a relative error of at most 0.015.
Values may be sent and summed in bfloat16 or wider, within the bound.
No kernel may reach another device: no remote copies, remote signals or barrier semaphores. Data moves between devices by JAX's collectives and lax.ppermute only.
A program may use at most 192 MiB of HBM per device.

v0:
```python
from functools import partial, reduce

import jax
import jax.numpy as jnp
from jax import lax
from jax.experimental import pallas as pl
from jax.experimental.pallas import tpu as pltpu
from jax.sharding import PartitionSpec as P

HEADS = 12
HEAD_DIM = 64
EPS = 1e-06
LIMITS = (12, 16, 23, 32, 46, 64, 91)
SCALE = 0.125
HIGH = lax.Precision.HIGHEST
LOW = jnp.bfloat16
FULL = jnp.float32
ROWS = 128
VMEM_BYTES = 52 * 1024 * 1024


def bucket_index(relative):
    distance = jnp.abs(relative)
    far_bucket = reduce(
        lambda counted, boundary: counted + (distance >= boundary).astype(jnp.int32),
        LIMITS,
        jnp.full_like(distance, 8),
    )
    return jnp.where(distance < 8, distance, far_bucket) + 16 * (relative > 0).astype(jnp.int32)


def segment_ids(lengths, slots):
    ending = jnp.cumsum(lengths)
    places = jnp.arange(slots, dtype=jnp.int32)
    return jnp.sum((places[:, None] >= ending[None, :]).astype(jnp.int32), axis=1)


def rms_parts(values, gain):
    inverse = lax.rsqrt(jnp.mean(values * values, axis=-1, keepdims=True) + EPS)
    return (values * inverse * gain, inverse)


def norm_back(values, inverse, gain, upstream):
    scaled = upstream * gain
    grad_values = inverse * scaled - values * inverse * inverse * inverse * jnp.mean(
        values * scaled, axis=-1, keepdims=True
    )
    return (grad_values, jnp.sum(upstream * values * inverse, axis=0))


def softmax_rows(scores):
    highest = jnp.max(scores, axis=-1, keepdims=True)
    raised = jnp.exp(scores - highest)
    return raised / jnp.sum(raised, axis=-1, keepdims=True)


def mm(left, right, contract, out=FULL):
    return lax.dot_general(left, right, (contract, ((), ())), preferred_element_type=FULL).astype(
        out
    )


def small_cost(flops, bytes_accessed, transcendentals):
    return pl.CostEstimate(
        flops=flops // 64,
        bytes_accessed=bytes_accessed // 64,
        transcendentals=transcendentals // 64,
    )


def nothing_kernel(*refs):
    del refs


def after(values, deps):
    values, deps = list(values), list(deps)
    anywhere = pl.BlockSpec(memory_space=pl.ANY)
    return pl.pallas_call(
        nothing_kernel,
        in_specs=[anywhere] * (len(values) + len(deps)),
        out_specs=[anywhere] * len(values),
        out_shape=[jax.ShapeDtypeStruct(value.shape, value.dtype) for value in values],
        input_output_aliases={number: number for number in range(len(values))},
        name="after",
    )(*values, *deps)


def swap(value, dim):
    axis, mask = dim
    count = lax.axis_size(axis)
    return lax.ppermute(value, axis, [(i, i ^ mask) for i in range(count)])


def bit_of(dim):
    axis, mask = dim
    return (lax.axis_index(axis) & mask) != 0


def stage_pair(value, dim):
    other = swap(value, dim)
    return jnp.where(bit_of(dim), jnp.stack((other, value)), jnp.stack((value, other)))


def ring_shift(value, places, by):
    count = 2 * places
    return lax.ppermute(value, "fsdp", [(i, (i - 2 * by) % count) for i in range(count)])


def z_gather(value, places, place):
    parts = jnp.stack([value] + [ring_shift(value, places, by) for by in range(1, places)])
    return lax.dynamic_slice_in_dim(
        jnp.concatenate((parts, parts)), lax.rem(places - place, places), places, 0
    )


def z_groups(places):
    return [[2 * place + side for place in range(places)] for side in (0, 1)]


def gather_step(held, dim):
    keys = list(held)
    value = jnp.stack([held[key] for key in keys]) if len(keys) > 1 else held[keys[0]]
    return swap(value, dim)


def gather_join(held, dim, arrived):
    keys = list(held)
    joined = dict(held)
    for number, key in enumerate(keys):
        joined[tuple(sorted(key + (dim,)))] = arrived[number] if len(keys) > 1 else arrived
    return joined


def gather_blocks(value, dims):
    held = {(): value}
    for dim in dims:
        held = gather_join(held, dim, gather_step(held, dim))
    return held


def gather_halves(value, dims):
    half = value.shape[0] // 2
    held = [{(): value[:half]}, {(): value[half:]}]
    brought = []
    for number in range(len(dims)):
        steps = (dims[number], dims[len(dims) - 1 - number])
        arrived = after([gather_step(part, dim) for part, dim in zip(held, steps)], ())
        brought.append(arrived)
        held = [gather_join(*of) for of in zip(held, steps, arrived)]
    upper, lower = held
    blocks = jnp.stack([jnp.concatenate((upper[key], lower[key])) for key in sorted(upper)])
    return (blocks, brought)


def scatter_halves(blocks, keys, dims):
    half = blocks.shape[1] // 2
    parts = [
        {key: blocks[number, :half] for number, key in enumerate(keys)},
        {key: blocks[number, half:] for number, key in enumerate(keys)},
    ]
    for number in range(len(dims)):
        steps = (dims[len(dims) - 1 - number], dims[number])
        stay = [[key for key in held if dim not in key] for held, dim in zip(parts, steps)]
        sent = [
            jnp.stack([held[tuple(sorted(key + (dim,)))].astype(LOW) for key in some])
            for held, dim, some in zip(parts, steps, stay)
        ]
        arrived = after([swap(value, dim) for value, dim in zip(sent, steps)], ())
        parts = [
            {
                key: held[key].astype(FULL) + value[place].astype(FULL)
                for place, key in enumerate(some)
            }
            for held, value, some in zip(parts, arrived, stay)
        ]
    return jnp.concatenate((parts[0][()], parts[1][()]))


def dense_gather(value, places, place, dims, core):
    columns = value.shape[1]
    half = (columns // 256) * 128
    near = z_gather(value, places, place)
    wanted = ("z", dims[0]) + tuple(sorted(dims[1:], reverse=True)) + ("core", "rows", "columns")

    def run(part, order):
        axes = ("z", "rows", "columns")
        for dim in order:
            part = stage_pair(part, dim)
            axes = (dim,) + axes
        part = stage_pair(part, core)
        axes = ("core",) + axes
        return part.transpose([axes.index(name) for name in wanted]).reshape(-1, part.shape[-1])

    first = run(near[..., :half], dims)
    second = run(near[..., half:], list(reversed(dims)))
    return (jnp.concatenate((first, second), axis=1), near)


def halve(parts, all_names, dims, beside=()):
    kept, sent, left = [], [], []
    for part, names, dim in zip(parts, all_names, dims):
        spot = names.index(dim)
        own = bit_of(dim).astype(jnp.int32)
        kept.append(lax.dynamic_index_in_dim(part, own, spot, keepdims=False))
        send = lax.dynamic_index_in_dim(part, 1 - own, spot, keepdims=False)
        sent.append(swap(send, dim))
        left.append(names[:spot] + names[spot + 1 :])
    arrived = after(sent + list(beside), ())
    sums = [(a.astype(FULL) + b.astype(FULL)).astype(LOW) for a, b in zip(kept, arrived)]
    return (sums, left, arrived[len(sent) :])


def add_up(value, others):
    return reduce(lambda total, other: total + other, others, value)


def dense_scatter(parts, names, orders, groups, small):
    all_names = [names] * len(parts)
    places = len(groups[0])
    for number, dims in enumerate(zip(*orders)):
        beside = ()
        if number == 0:
            beside = [swap(small, ("dp", mask)) for mask in range(1, lax.axis_size("dp"))]
        elif number == 1:
            beside = [swap(small, ("fsdp", 1))]
        parts, all_names, others = halve(parts, all_names, dims, beside)
        small = add_up(small, others)
    joined = jnp.concatenate(parts, axis=-1)
    moved = lax.all_to_all(
        joined, "fsdp", split_axis=0, concat_axis=0, axis_index_groups=groups, tiled=True
    )
    near = [ring_shift(small, places, by) for by in range(1, places)]
    moved, *others = after([moved] + near, ())
    return (jnp.sum(moved.astype(FULL), axis=0), add_up(small, others))


def diagonal_hot(slots, bucket_count):
    width = 2 * slots
    lanes = jnp.arange(width, dtype=jnp.int32)[None, :]
    rows = jnp.arange(8, dtype=jnp.int32)[:, None]
    diagonal = (lanes - rows + (ROWS - 1)) % width
    bucket = jnp.where(diagonal < width - 1, bucket_index(diagonal - (slots - 1)), -1)
    return (bucket[:, :, None] == jnp.arange(bucket_count, dtype=jnp.int32)).astype(FULL)


def attend_kernel(query, key, value, base, seg_col, seg_row, out, probs, toeplitz):
    slots = query.shape[0]
    lanes = lax.broadcasted_iota(jnp.int32, (1, 2 * HEAD_DIM), 1)
    total = [None] * (slots // ROWS)
    for head in range(2):
        mine = (lanes >= head * HEAD_DIM) & (lanes < (head + 1) * HEAD_DIM)
        table = base[head]
        size = 8
        while size < ROWS:
            table = jnp.concatenate((table, pltpu.roll(table, size, 1)), axis=0)
            size *= 2
        toeplitz[...] = table
        value_head = jnp.where(mine, value[...], 0).astype(LOW)
        for block in range(slots // ROWS):
            rows = pl.ds(block * ROWS, ROWS)
            query_head = jnp.where(mine, query[rows, :], 0).astype(LOW)
            shift = slots - ROWS - block * ROWS
            scores = mm(query_head, key[...], ((1,), (1,))) * SCALE
            scores = scores + toeplitz[:, shift : shift + slots]
            scores = jnp.where(seg_col[rows, :] == seg_row[...], scores, -1e30)
            highest = jnp.max(scores, axis=-1, keepdims=True)
            raised = jnp.exp(scores - highest)
            low = (raised / jnp.sum(raised, axis=-1, keepdims=True)).astype(LOW)
            probs[head, rows, :] = low
            part = mm(low, value_head, ((1,), (0,)))
            total[block] = part if head == 0 else total[block] + part
    for block in range(slots // ROWS):
        out[pl.ds(block * ROWS, ROWS), :] = total[block].astype(LOW)


def attend_forward(projected, base, seg_col, seg_row):
    slots = projected.shape[0]
    width = projected.shape[1] // 3
    pairs = HEADS // 2
    lanes = 2 * HEAD_DIM
    return pl.pallas_call(
        attend_kernel,
        grid=(pairs,),
        in_specs=[
            pl.BlockSpec((slots, lanes), lambda p: (0, p)),
            pl.BlockSpec((slots, lanes), lambda p: (0, p + pairs)),
            pl.BlockSpec((slots, lanes), lambda p: (0, p + 2 * pairs)),
            pl.BlockSpec((2, 8, 2 * slots), lambda p: (p, 0, 0)),
            pl.BlockSpec((slots, 1), lambda p: (0, 0)),
            pl.BlockSpec((1, slots), lambda p: (0, 0)),
        ],
        out_specs=[
            pl.BlockSpec((slots, lanes), lambda p: (0, p)),
            pl.BlockSpec((2, slots, slots), lambda p: (p, 0, 0)),
        ],
        out_shape=[
            jax.ShapeDtypeStruct((slots, width), LOW),
            jax.ShapeDtypeStruct((HEADS, slots, slots), LOW),
        ],
        scratch_shapes=[pltpu.VMEM((ROWS, 2 * slots), FULL)],
        compiler_params=pltpu.CompilerParams(vmem_limit_bytes=VMEM_BYTES),
        cost_estimate=small_cost(
            flops=HEADS * slots * slots * HEAD_DIM * 16,
            bytes_accessed=HEADS * slots * slots * 2 + 8 * slots * width,
            transcendentals=HEADS * slots * slots,
        ),
        name="attend_forward",
    )(projected, projected, projected, base, seg_col, seg_row)


def attend_back_kernel(
    query, key, value, grad, probs, out_query, out_key, out_value, diagonals, lined, scores_low
):
    slots = query.shape[0]
    lanes = lax.broadcasted_iota(jnp.int32, (1, 2 * HEAD_DIM), 1)
    query_total = [None] * (slots // ROWS)
    key_total = value_total = None
    for head in range(2):
        mine = (lanes >= head * HEAD_DIM) & (lanes < (head + 1) * HEAD_DIM)
        key_head = jnp.where(mine, key[...], 0).astype(LOW)
        grad_head = jnp.where(mine, grad[...], 0).astype(LOW)
        query_head = jnp.where(mine, query[...], 0).astype(LOW)
        lined[...] = jnp.zeros_like(lined)
        for block in range(slots // ROWS):
            rows = pl.ds(block * ROWS, ROWS)
            soft = probs[head, rows, :].astype(FULL)
            grad_rows = jnp.where(mine, grad[rows, :], 0).astype(LOW)
            weighted = soft * mm(grad_rows, value[...], ((1,), (1,)))
            back = weighted - soft * jnp.sum(weighted, axis=-1, keepdims=True)
            low = back.astype(LOW)
            scores_low[rows, :] = low
            shift = slots - ROWS - block * ROWS
            lined[:, shift : shift + slots] += low.astype(FULL)
            part = mm(low, key_head, ((1,), (0,)))
            query_total[block] = part if head == 0 else query_total[block] + part
        key_part = mm(scores_low[...], query_head, ((0,), (0,)))
        value_part = mm(probs[head], grad_head, ((0,), (0,)))
        key_total = key_part if head == 0 else key_total + key_part
        value_total = value_part if head == 0 else value_total + value_part
        table = lined[...]
        size = ROWS
        while size > 8:
            size //= 2
            table = table[:size] + pltpu.roll(table[size:], 2 * slots - size, 1)
        diagonals[head] = table
    out_key[...] = (key_total * SCALE).astype(LOW)
    out_value[...] = value_total.astype(LOW)
    for block in range(slots // ROWS):
        out_query[pl.ds(block * ROWS, ROWS), :] = (query_total[block] * SCALE).astype(LOW)


def attend_back(projected, grad_attended, probs, begin, count):
    slots = projected.shape[0]
    pairs = HEADS // 2
    lanes = 2 * HEAD_DIM
    width = count * lanes
    column = pl.BlockSpec((slots, lanes), lambda p: (0, p))

    def column_from(offset):
        return pl.BlockSpec((slots, lanes), lambda p: (0, p + offset))

    return pl.pallas_call(
        attend_back_kernel,
        grid=(count,),
        in_specs=[
            column_from(begin),
            column_from(begin + pairs),
            column_from(begin + 2 * pairs),
            column_from(begin),
            pl.BlockSpec((2, slots, slots), lambda p: (p + begin, 0, 0)),
        ],
        out_specs=[
            column,
            column,
            column,
            pl.BlockSpec((2, 8, 2 * slots), lambda p: (p, 0, 0)),
        ],
        out_shape=[jax.ShapeDtypeStruct((slots, width), LOW)] * 3
        + [jax.ShapeDtypeStruct((2 * count, 8, 2 * slots), FULL)],
        scratch_shapes=[pltpu.VMEM((ROWS, 2 * slots), FULL), pltpu.VMEM((slots, slots), LOW)],
        compiler_params=pltpu.CompilerParams(vmem_limit_bytes=VMEM_BYTES),
        cost_estimate=small_cost(
            flops=2 * count * slots * slots * HEAD_DIM * 32,
            bytes_accessed=2 * count * slots * slots * 2 + 14 * slots * width,
            transcendentals=0,
        ),
        name="attend_back",
    )(projected, projected, projected, grad_attended, probs)


def second_of(weights):
    _, rows, units = weights.shape
    width = rows // 2
    runs = [weights[0, row : row + units, :] for row in range(width, rows, units)]
    return jnp.concatenate(runs, axis=1)


def expert_kernel(
    rows, grads, weights, y_out, back_out, weights_out, y_sum, back_sum, hidden_low, pre_low
):
    chunk = pl.program_id(0)
    count, width = rows.shape[1:]
    units = weights.shape[2]
    step = min(256, count)
    second = second_of(weights)

    @pl.when(chunk == 0)
    def _():
        y_sum[...] = jnp.zeros_like(y_sum)
        back_sum[...] = jnp.zeros_like(back_sum)

    for block in range(count // step):
        some = pl.ds(block * step, step)
        pre = mm(rows[0, some, :], weights[0, :width, :], ((1,), (0,)))
        grad_hidden = mm(grads[0, some, :], second, ((1,), (1,)))
        normal_cdf = 0.5 + 0.5 * lax.erf(pre * 0.7071067811865476)
        slope = normal_cdf + pre * jnp.exp(-0.5 * pre * pre) * 0.3989422804014327
        hidden = (pre * normal_cdf).astype(LOW)
        grad_pre = (grad_hidden * slope).astype(LOW)
        hidden_low[some, :] = hidden
        pre_low[some, :] = grad_pre
        y_sum[some, :] += mm(hidden, second, ((1,), (0,)))
        back_sum[some, :] += mm(grad_pre, weights[0, :width, :], ((1,), (1,)))
    weights_out[0, :width, :] = mm(rows[0], pre_low[...], ((0,), (0,)), LOW)
    second_grad = mm(hidden_low[...], grads[0], ((0,), (0,)), LOW)
    for column in range(0, width, units):
        weights_out[0, width + column : width + column + units, :] = second_grad[
            :, column : column + units
        ]

    @pl.when(chunk == pl.num_programs(0) - 1)
    def _():
        y_out[...] = y_sum[...].astype(LOW)
        back_out[...] = back_sum[...].astype(LOW)


def run_expert(expert, rows, grads, weights):
    chunks, height, units = weights.shape
    count, width = rows.shape[1:]
    rows_in = pl.BlockSpec((1, count, width), lambda c: (expert, 0, 0))
    rows_out = pl.BlockSpec((count, width), lambda c: (0, 0))
    weight_spec = pl.BlockSpec((1, height, units), lambda c: (c, 0, 0))
    rows_shape = jax.ShapeDtypeStruct((count, width), LOW)
    return pl.pallas_call(
        expert_kernel,
        grid=(chunks,),
        in_specs=[rows_in, rows_in, weight_spec],
        out_specs=[rows_out, rows_out, weight_spec],
        out_shape=[rows_shape, rows_shape, jax.ShapeDtypeStruct(weights.shape, LOW)],
        scratch_shapes=[
            pltpu.VMEM((count, width), FULL),
            pltpu.VMEM((count, width), FULL),
            pltpu.VMEM((count, units), LOW),
            pltpu.VMEM((count, units), LOW),
        ],
        compiler_params=pltpu.CompilerParams(vmem_limit_bytes=VMEM_BYTES),
        cost_estimate=small_cost(
            flops=chunks * 12 * count * width * units,
            bytes_accessed=8 * count * width + 8 * chunks * width * units,
            transcendentals=2 * chunks * count * units,
        ),
        name="run_expert",
    )(rows, grads, weights)


def place_kernel(groups, hot, *refs):
    *parts, out = refs
    size = len(parts) // groups
    width = parts[0].shape[1]
    for group in range(groups):
        some = [part[...] for part in parts[group * size : (group + 1) * size]]
        values = jnp.concatenate(some, axis=0)
        out[0, :, group * width : (group + 1) * width] = mm(hot[0], values, ((1,), (0,)), LOW)


def place_rows(hot, groups, capacity):
    blocks, count, slots = hot.shape
    parts = sum(groups, [])
    width = parts[0].shape[1]
    wide = width * len(groups)
    return pl.pallas_call(
        partial(place_kernel, len(groups)),
        grid=(blocks,),
        in_specs=[pl.BlockSpec((1, count, slots), lambda b: (b, 0, 0))]
        + [pl.BlockSpec((capacity, width), lambda b: (b, 0))] * len(parts),
        out_specs=pl.BlockSpec((1, count, wide), lambda b: (b, 0, 0)),
        out_shape=jax.ShapeDtypeStruct((blocks, count, wide), LOW),
        compiler_params=pltpu.CompilerParams(vmem_limit_bytes=VMEM_BYTES),
        cost_estimate=small_cost(
            flops=2 * blocks * count * slots * wide,
            bytes_accessed=4 * blocks * count * wide,
            transcendentals=0,
        ),
        name="place_rows",
    )(hot, *parts)


def body(
    tokens,
    cotangent,
    seq_lens,
    routes,
    norm_gains,
    qkv_weight,
    out_weight,
    router_weight,
    rel_bias,
    expert_in,
    expert_out,
):
    tok_count, width = tokens.shape
    bucket_count = rel_bias.shape[0]
    shard_rows = qkv_weight.shape[0]
    experts_all = router_weight.shape[1]
    local_experts, _, units = expert_in.shape
    capacity = 2 * tok_count // experts_all
    places = lax.axis_size("fsdp") // 2
    place = lax.axis_index("fsdp") // 2
    peer = lax.axis_index("dp")
    peer_count = lax.axis_size("dp")
    core = ("dp", 1)
    dims = [("fsdp", 1)]
    mask = 2
    while mask < peer_count:
        dims.append(("dp", mask))
        mask *= 2

    spare = -(4 * width + experts_all + 2) % 128
    packed = jnp.concatenate(
        (
            qkv_weight,
            out_weight,
            router_weight,
            norm_gains.T,
            jnp.zeros((shard_rows, spare), LOW),
        ),
        axis=1,
    )
    dense, near = dense_gather(packed, places, place, dims, core)
    qkv_full = dense[:, : 3 * width]
    out_full = dense[:, 3 * width : 4 * width]
    router_full = dense[:, 4 * width : 4 * width + experts_all]
    gains_float = dense[:, 4 * width + experts_all : 4 * width + experts_all + 2].T.astype(FULL)

    groups = z_groups(places)
    weights = []
    for expert in range(local_experts):
        runs = [expert_out[expert][:, row : row + units] for row in range(0, width, units)]
        own = jnp.concatenate([expert_in[expert]] + runs)
        if expert > 0:
            (own,) = after((own,), (near,))
        weights.append(lax.all_gather(own, "fsdp", axis=0, axis_index_groups=groups))

    chosen = routes[:, 0]
    chosen_hot = chosen[:, None] == jnp.arange(experts_all, dtype=jnp.int32)[None, :]
    order = jnp.arange(tok_count, dtype=jnp.int32)
    earlier = (order[:, None] > order[None, :]).astype(LOW)
    rank_all = jnp.dot(earlier, chosen_hot.astype(LOW), preferred_element_type=FULL)
    rank_in = jnp.sum(jnp.where(chosen_hot, rank_all, 0.0), axis=1).astype(jnp.int32)
    slots_of = gather_blocks((chosen * capacity + rank_in)[None, :], dims)
    keys = sorted(slots_of)
    slots_near = jnp.stack([slots_of[key][0] for key in keys])
    local_slots = local_experts * capacity
    slot_ids = jnp.arange(local_slots, dtype=jnp.int32).reshape(local_experts, capacity)

    def hot_of(owner):
        wanted = owner * local_slots + slot_ids
        return (slots_near[:, None, None, :] == wanted[None, :, :, None]).astype(LOW)

    hot_own, hot_other = hot_of(peer), hot_of(peer ^ 1)
    segment = segment_ids(seq_lens[0], tok_count)
    bucket_hot = diagonal_hot(tok_count, bucket_count)
    base = jnp.einsum("rjb,bh->hrj", bucket_hot, rel_bias, precision=HIGH)

    inputs = tokens.astype(FULL)
    normed_one, inverse_one = rms_parts(inputs, gains_float[0])
    normed_low = normed_one.astype(LOW)
    projected = jnp.dot(normed_low, qkv_full, preferred_element_type=FULL).astype(LOW)
    attended, probs = attend_forward(projected, base, segment[:, None], segment[None, :])
    hidden_one = inputs + jnp.dot(attended, out_full, preferred_element_type=FULL)
    normed_two, inverse_two = rms_parts(hidden_one, gains_float[1])
    normed_two_low = normed_two.astype(LOW)
    router_soft = softmax_rows(jnp.dot(normed_two_low, router_full, preferred_element_type=FULL))
    gate_value = jnp.sum(jnp.where(chosen_hot, router_soft, 0.0), axis=1)
    upstream = cotangent.astype(FULL)
    grad_y = (gate_value[:, None] * upstream).astype(LOW)

    def pick(hot, blocks):
        return jnp.einsum("bjst,btd->jbsd", hot, blocks, preferred_element_type=FULL).astype(LOW)

    def to_rows(blocks):
        other = swap(pick(hot_other, blocks), core)
        both = jnp.stack((pick(hot_own, blocks), other), axis=1)
        return both.reshape(local_experts, -1, width)

    token_ids = jnp.concatenate((peer * local_slots + slot_ids, (peer ^ 1) * local_slots + slot_ids))
    hot_back = (slots_near[:, :, None] == token_ids.reshape(-1)[None, None, :]).astype(LOW)

    def from_rows(*groups):
        near_rows = len(keys) * capacity
        parts = [
            list(values) + [swap(value[near_rows:], core) for value in values] for values in groups
        ]
        return place_rows(hot_back, parts, capacity)

    blocks, brought = gather_halves(normed_two_low, dims)
    rows = to_rows(blocks)
    (grad_tied,) = after((grad_y,), brought[0])
    grad_blocks, _ = gather_halves(grad_tied, dims)
    grads = to_rows(grad_blocks)
    results = []
    for expert in range(local_experts):
        held = weights[expert]
        if expert > 0:
            (held,) = after((held,), (results[-1][0], hot_back))
        results.append(run_expert(expert, rows, grads, held))
    summed = [
        lax.psum_scatter(
            result[2], "fsdp", scatter_dimension=0, axis_index_groups=groups, tiled=False
        )
        for result in results
    ]
    returned = scatter_halves(
        from_rows(*[[result[which] for result in results] for which in (0, 1)]), keys, dims
    )
    token_y, grad_rows = returned[:, :width], returned[:, width:]

    mixed = (hidden_one + gate_value[:, None] * token_y).astype(LOW)
    grad_gate = jnp.sum(upstream * token_y, axis=1)
    grad_logits = router_soft * (
        jnp.where(chosen_hot, grad_gate[:, None], 0.0) - (gate_value * grad_gate)[:, None]
    )
    router_local = jnp.dot(normed_two_low.astype(FULL).T, grad_logits, precision=HIGH)
    grad_normed_two = grad_rows + jnp.dot(
        grad_logits, router_full.astype(FULL).T, precision=HIGH
    )
    grad_from_two, gain_grad_two = norm_back(
        hidden_one, inverse_two, gains_float[1], grad_normed_two
    )
    grad_hidden_one = upstream + grad_from_two
    grad_attn_low = grad_hidden_one.astype(LOW)
    out_local = jnp.einsum("td,te->de", attended, grad_attn_low, preferred_element_type=FULL)
    grad_attended = mm(grad_attn_low, out_full, ((1,), (1,)), LOW)
    names = ["z", dims[0]] + sorted(dims[1:], reverse=True) + [core]

    def split_rows(panel):
        shape = (places,) + (2,) * (len(names) - 1) + (shard_rows, panel.shape[1])
        parts, left, _ = halve([panel.reshape(shape)], [names], [core])
        return (parts[0], left[0])

    spare_out = -(experts_all + 2) % 128
    out_panel = jnp.concatenate(
        (
            out_local.astype(LOW),
            router_local.astype(LOW),
            gain_grad_two[:, None].astype(LOW),
            jnp.zeros((width, spare_out + 1), LOW),
        ),
        axis=1,
    )
    out_half, half_names = split_rows(out_panel)
    early = summed[:-1]
    (grad_attended,) = after((grad_attended,), early)
    *grad_parts, diagonals = attend_back(projected, grad_attended, probs, 0, HEADS // 2)
    grad_projected = jnp.concatenate(grad_parts, axis=1)
    qkv_local = mm(normed_low, grad_projected, ((0,), (0,)), LOW)
    qkv_half, _ = split_rows(qkv_local)
    half = 3 * width // 2
    grad_normed_one = mm(grad_projected, qkv_full, ((1,), (1,)))
    grad_from_one, gain_grad_one = norm_back(inputs, inverse_one, gains_float[0], grad_normed_one)
    tokens_grad = grad_hidden_one + grad_from_one
    bias_local = jnp.einsum("hrj,rjb->bh", diagonals, bucket_hot, precision=HIGH)
    gain_rows = width // 128
    small = jnp.concatenate((bias_local.reshape(-1, 128), gain_grad_one.reshape(-1, 128)))
    dense_sum, small = dense_scatter(
        [qkv_half[..., :half], qkv_half[..., half:], out_half],
        half_names,
        [dims, dims[::-1], dims[::-1]],
        groups,
        small,
    )
    summed[-1:] = after(summed[-1:], (dense_sum,))
    in_grad = jnp.stack([both[:width].astype(FULL) for both in summed])
    out_expert_grad = jnp.stack(
        [
            jnp.concatenate(
                [both[row : row + units].astype(FULL) for row in range(width, 2 * width, units)],
                axis=1,
            )
            for both in summed
        ]
    )
    qkv_grad, out_sum = dense_sum[:, : 3 * width], dense_sum[:, 3 * width :]
    bias_grad = small[:-gain_rows].reshape(bias_local.shape)
    device = lax.axis_index("fsdp") * peer_count + peer
    gain_one = lax.dynamic_slice_in_dim(
        small[-gain_rows:].reshape(-1), device * shard_rows, shard_rows
    )
    gains_grad = jnp.stack((gain_one, out_sum[:, width + experts_all]))
    router_grad = out_sum[:, width : width + experts_all]
    out_grad = out_sum[:, :width]
    return (
        mixed,
        tokens_grad,
        gains_grad,
        qkv_grad,
        out_grad,
        router_grad,
        bias_grad,
        in_grad,
        out_expert_grad,
    )


def solution(mesh):
    rows = P(("fsdp", "dp"), None)
    columns = P(None, ("fsdp", "dp"))
    experts = (P("dp", None, "fsdp"), P("dp", "fsdp", None))
    return jax.shard_map(
        body,
        mesh=mesh,
        in_specs=(rows, rows, rows, rows, columns, rows, rows, rows, P()) + experts,
        out_specs=(rows, rows, columns, rows, rows, rows, P()) + experts,
        check_vma=False,
    )
```

profile of v0, /device:TPU:0, one launch (start us, length us, event | category | flops | bytes accessed | tf_op | source)
XLA Modules:
  0.0 425.3 jit_solution(16829955953089608218)
XLA Ops:
  9.8 5.1 %collective-permute-start = (bf16[24,3200]{1,0:T(8,128)(2,1)S(1)}, bf16[24,3200]{1,0:T(8,128)(2,1)S(1)}, u32[]{:S(2)}, u32[]{:S(2)}) collective-permute-start(bf16[24,3200]{1,0:T(8,128)(2,1)S(1)} %concatenate.159), channel_id=1, source_target_pairs={{0,24},{4,28},{8,0},{12,4},{16,8},{20,12},{24,16},{28,20},{1,25},{... | collective-permute-start | bytes 460808 | tf_op jit(solution)/shard_map/ppermute | solution.py:106
  24.1 2.2 pad_maximum_fusion.8.refs_0_
  45.2 4.0 collective-permute-done.3
  52.3 6.7 %collective-permute-done.7 = bf16[2,4,24,1536]{3,2,1,0:T(8,128)(2,1)S(1)} collective-permute-done((bf16[2,4,24,1536]{3,2,1,0:T(8,128)(2,1)S(1)}, bf16[2,4,24,1536]{3,2,1,0:T(8,128)(2,1)S(1)}, u32[]{:S(2)}, u32[]{:S(2)}) %collective-permute-start.7) | collective-permute-done | bytes 589856 | tf_op jit(solution)/shard_map/ppermute | solution.py:91
  65.3 3.5 convolution_convert_fusion.1.query.key.value
  68.9 15.4 %attend_forward.1 = (bf16[512,768]{1,0:T(8,128)(2,1)S(1)}, bf16[12,512,512]{2,1,0:T(8,128)(2,1)}) custom-call(bf16[512,2304]{1,0:T(8,128)(2,1)} %convolution_convert_fusion.1.query.key.value, bf16[512,2304]{1,0:T(8,128)(2,1)} %convolution_convert_fusion.1.query.key.value, bf16[512,2304]{1,0:T(8,128)(2,1)} %convolution_convert_fusion.1.query.key.value, ...), custom_call_target="tpu_custom_call" | custom-call | flops 50331648 | bytes 147456 | tf_op jit(solution)/shard_map/attend_forward/pallas_call | solution.py:281
  92.1 5.4 %collective-permute-done.11.refs_0_ = bf16[256,768]{1,0:T(8,128)(2,1)S(1)} collective-permute-done((bf16[256,768]{1,0:T(8,128)(2,1)S(1)}, bf16[256,768]{1,0:T(8,128)(2,1)S(1)}, u32[]{:S(2)}, u32[]{:S(2)}) %collective-permute-start.11) | collective-permute-done | bytes 393248 | tf_op jit(solution)/shard_map/ppermute | solution.py:91
  109.9 18.2 %collective-permute-done.16.refs_0_ = bf16[256,768]{1,0:T(8,128)(2,1)} collective-permute-done((bf16[256,768]{1,0:T(8,128)(2,1)S(1)}, bf16[256,768]{1,0:T(8,128)(2,1)}, u32[]{:S(2)}, u32[]{:S(2)}) %collective-permute-start.16) | collective-permute-done | bytes 393248 | tf_op jit(solution)/shard_map/ppermute | solution.py:91
  128.1 3.2 collective-permute-done.17.refs_1_
  142.0 2.4 fusion.42
  144.4 6.8 %collective-permute-done.19.refs_1_ = bf16[2,256,768]{2,1,0:T(8,128)(2,1)S(1)} collective-permute-done((bf16[2,256,768]{2,1,0:T(8,128)(2,1)}, bf16[2,256,768]{2,1,0:T(8,128)(2,1)S(1)}, u32[]{:S(2)}, u32[]{:S(2)}) %collective-permute-start.19) | collective-permute-done | bytes 786464 | tf_op jit(solution)/shard_map/ppermute | solution.py:91
  151.2 3.0 collective-permute-done.18.refs_0_
  158.3 2.5 fusion.39
  160.8 2.8 fusion.48
  172.8 24.4 %run_expert.2 = (bf16[1024,768]{1,0:T(8,128)(2,1)S(1)}, bf16[1024,768]{1,0:T(8,128)(2,1)}, bf16[4,1536,384]{2,1,0:T(8,128)(2,1)}) custom-call(bf16[2,1024,768]{2,1,0:T(8,128)(2,1)} %bitcast.233, bf16[2,1024,768]{2,1,0:T(8,128)(2,1)} %bitcast.235, bf16[4,1536,384]{2,1,0:T(8,128)(2,1)} %bitcast.244), custom_call_target="tpu_custom_call" | custom-call | flops 226492416 | bytes 245760 | tf_op jit(solution)/shard_map/run_expert/pallas_call | solution.py:444
  201.8 24.4 %run_expert.3 = (bf16[1024,768]{1,0:T(8,128)(2,1)S(1)}, bf16[1024,768]{1,0:T(8,128)(2,1)}, bf16[4,1536,384]{2,1,0:T(8,128)(2,1)}) custom-call(bf16[2,1024,768]{2,1,0:T(8,128)(2,1)} %bitcast.234, bf16[2,1024,768]{2,1,0:T(8,128)(2,1)} %bitcast.236, bf16[4,1536,384]{2,1,0:T(8,128)(2,1)} %after.22.weights), custom_call_target="tpu_custom_call" | custom-call | flops 226492416 | bytes 245760 | tf_op jit(solution)/shard_map/run_expert/pallas_call | solution.py:444
  231.6 8.3 %place_rows.1 = bf16[4,512,1536]{2,1,0:T(8,128)(2,1)} custom-call(bf16[4,512,512]{2,1,0:T(8,128)(2,1)} %compare_convert_fusion.refs_2_.hot, bf16[1024,768]{1,0:T(8,128)(2,1)} %copy-done.2, bf16[1024,768]{1,0:T(8,128)(2,1)} %copy-done.3, bf16[512,768]{1,0:T(8,128)(2,1)S(1)} %collective-permute-done.21.refs_2_, ...), custom_call_target="tpu_custom_call" | custom-call | flops 50331648 | bytes 196608 | tf_op jit(solution)/shard_map/place_rows/pallas_call | solution.py:481
  245.5 34.3 %collective-permute-done.26.refs_1_ = bf16[2,256,1536]{2,1,0:T(8,128)(2,1)S(1)} collective-permute-done((bf16[2,256,1536]{2,1,0:T(8,128)(2,1)S(1)}, bf16[2,256,1536]{2,1,0:T(8,128)(2,1)S(1)}, u32[]{:S(2)}, u32[]{:S(2)}) %collective-permute-start.26) | collective-permute-done | bytes 1572896 | tf_op jit(solution)/shard_map/ppermute | solution.py:91
  281.0 3.4 add_convert_fusion.1
  287.3 16.4 %collective-permute-done.27.refs_0_ = bf16[1,256,1536]{2,1,0:T(8,128)(2,1)} collective-permute-done((bf16[1,256,1536]{2,1,0:T(8,128)(2,1)}, bf16[1,256,1536]{2,1,0:T(8,128)(2,1)}, u32[]{:S(2)}, u32[]{:S(2)}) %collective-permute-start.27) | collective-permute-done | bytes 786464 | tf_op jit(solution)/shard_map/ppermute | solution.py:91
  304.0 2.8 add_bitcast_fusion.1
  314.8 16.5 %attend_back.1 = (bf16[512,768]{1,0:T(8,128)(2,1)S(1)}, bf16[512,768]{1,0:T(8,128)(2,1)S(1)}, bf16[512,768]{1,0:T(8,128)(2,1)}, f32[12,8,1024]{2,1,0:T(8,128)S(1)}) custom-call(bf16[512,2304]{1,0:T(8,128)(2,1)} %convolution_convert_fusion.1.query.key.value, bf16[512,2304]{1,0:T(8,128)(2,1)} %convolution_convert_fusion.1.query.key.value, ...), custom_call_target="tpu_custom_call" | custom-call | flops 100663296 | bytes 184320 | tf_op jit(solution)/shard_map/attend_back/pallas_call | solution.py:362
  332.7 2.1 convolution_convert_fusion
  334.8 2.1 dynamic-slice_bitcast_fusion
  347.3 2.6 fusion
  354.0 3.8 fusion.36
  360.7 5.4 %collective-permute-done.35.refs_4_ = f32[9,128]{1,0:T(8,128)S(1)} collective-permute-done((f32[9,128]{1,0:T(8,128)S(1)}, f32[9,128]{1,0:T(8,128)S(1)}, u32[]{:S(2)}, u32[]{:S(2)}) %collective-permute-start.35) | collective-permute-done | bytes 4640 | tf_op jit(solution)/shard_map/ppermute | solution.py:91
  377.6 2.6 collective-permute-done.40.refs_3_
  386.3 4.3 %all-to-all-start = ((bf16[4,24,3200]{2,1,0:T(8,128)(2,1)}), bf16[4,24,3200]{2,1,0:T(8,128)(2,1)S(1)}, u32[]{:S(2)}, u32[]{:S(2)}) async-start(bf16[4,24,3200]{2,1,0:T(8,128)(2,1)} %pad_maximum_fusion.13), calls=%async_computation.1 | async-start | bytes 1228800 | tf_op jit(solution)/shard_map/all_to_all | solution.py:229
  391.8 3.1 fusion.30
  394.9 3.9 collective-permute-start.41
  400.2 6.6 %collective-permute-done.42.refs_2_ = f32[9,128]{1,0:T(8,128)S(1)} collective-permute-done((f32[9,128]{1,0:T(8,128)S(1)}, f32[9,128]{1,0:T(8,128)S(1)}, u32[]{:S(2)}, u32[]{:S(2)}) %collective-permute-start.42) | collective-permute-done | bytes 4640 | tf_op jit(solution)/shard_map/ppermute | solution.py:106
  (481 shorter events, 161.6 us)
Async XLA Ops:
  7.2 165.6 %all-gather.5.cloned.1.call-start = ((), (), s32[]{:S(2)}) async-start(), calls=%async_computation.5 | async-start | bytes 5898240 | tf_op jit(solution)/shard_map/all_gather | solution.py:552
  9.8 20.8 %collective-permute-start = (bf16[24,3200]{1,0:T(8,128)(2,1)S(1)}, bf16[24,3200]{1,0:T(8,128)(2,1)S(1)}, u32[]{:S(2)}, u32[]{:S(2)}) collective-permute-start(bf16[24,3200]{1,0:T(8,128)(2,1)S(1)} %concatenate.159), channel_id=1, source_target_pairs={{0,24},{4,28},{8,0},{12,4},{16,8},{20,12},{24,16},{28,20},{1,25},{... | collective-permute-start | bytes 460808 | tf_op jit(solution)/shard_map/ppermute | solution.py:106
  14.9 15.8 %collective-permute-start.1 = (bf16[24,3200]{1,0:T(8,128)(2,1)S(1)}, bf16[24,3200]{1,0:T(8,128)(2,1)}, u32[]{:S(2)}, u32[]{:S(2)}) collective-permute-start(bf16[24,3200]{1,0:T(8,128)(2,1)S(1)} %concatenate.159), channel_id=1, source_target_pairs={{0,16},{4,20},{8,24},{12,28},{16,0},{20,4},{24,8},{28,12},{1,17},{... | collective-permute-start | bytes 460808 | tf_op jit(solution)/shard_map/ppermute | solution.py:106
  14.9 16.7 %collective-permute-start.2 = (bf16[24,3200]{1,0:T(8,128)(2,1)S(1)}, bf16[24,3200]{1,0:T(8,128)(2,1)}, u32[]{:S(2)}, u32[]{:S(2)}) collective-permute-start(bf16[24,3200]{1,0:T(8,128)(2,1)S(1)} %concatenate.159), channel_id=1, source_target_pairs={{0,8},{4,12},{8,16},{12,20},{16,24},{20,28},{24,0},{28,4},{1,9},{5... | collective-permute-start | bytes 460808 | tf_op jit(solution)/shard_map/ppermute | solution.py:106
  17.7 8.7 %collective-permute-start.9 = (s32[1,512]{1,0:T(1,128)S(1)}, s32[1,512]{1,0:T(1,128)S(1)}, u32[]{:S(2)}, u32[]{:S(2)}) collective-permute-start(s32[1,512]{1,0:T(1,128)S(1)} %bitcast_add_fusion.1), channel_id=1, source_target_pairs={{0,4},{4,0},{8,12},{12,8},{16,20},{20,16},{24,28},{28,24},{1,5},{5... | collective-permute-start | bytes 6152 | tf_op jit(solution)/shard_map/ppermute | solution.py:91
  22.7 179.1 %all-gather.7.cloned.1.call-start = ((), (), s32[]{:S(2)}) async-start(), calls=%async_computation.6 | async-start | bytes 5898240 | tf_op jit(solution)/shard_map/all_gather | solution.py:552
  39.0 10.3 %collective-permute-start.3 = (bf16[4,24,1664]{2,1,0:T(8,128)(2,1)}, bf16[4,24,1664]{2,1,0:T(8,128)(2,1)S(1)}, u32[]{:S(2)}, u32[]{:S(2)}) collective-permute-start(bf16[4,24,1664]{2,1,0:T(8,128)(2,1)} %constant_dynamic-slice_fusion.1), channel_id=1, source_target_pairs={{0,2},{1,3},{2,0},{3,1},{4,6},{5,7},{6,4},{7,5},{8,10},{9,11},{10,... | collective-permute-start | bytes 958472 | tf_op jit(solution)/shard_map/ppermute | solution.py:91
  41.3 273.5 %reduce-scatter.3.cloned.1.call-start = ((), (), s32[]{:S(2)}) async-start(), calls=%async_computation.3 | async-start | bytes 5898240 | tf_op jit(solution)/shard_map/reduce_scatter | solution.py:618
  43.6 15.3 %collective-permute-start.7 = (bf16[2,4,24,1536]{3,2,1,0:T(8,128)(2,1)S(1)}, bf16[2,4,24,1536]{3,2,1,0:T(8,128)(2,1)S(1)}, u32[]{:S(2)}, u32[]{:S(2)}) collective-permute-start(bf16[2,4,24,1536]{3,2,1,0:T(8,128)(2,1)S(1)} %maximum_select_fusion.8), channel_id=1, source_target_pairs={{0,2},{1,3},{2,0},{3,1},{4,6},{5,7},{6,4},{7,5},{8,10},{9,11},{10,... | collective-permute-start | bytes 1769480 | tf_op jit(solution)/shard_map/ppermute | solution.py:91
  49.4 10.5 %collective-permute-start.4 = (bf16[2,4,24,1664]{3,2,1,0:T(8,128)(2,1)S(1)}, bf16[2,4,24,1664]{3,2,1,0:T(8,128)(2,1)S(1)}, u32[]{:S(2)}, u32[]{:S(2)}) collective-permute-start(bf16[2,4,24,1664]{3,2,1,0:T(8,128)(2,1)S(1)} %maximum_select_fusion.6), channel_id=1, source_target_pairs={{0,4},{4,0},{8,12},{12,8},{16,20},{20,16},{24,28},{28,24},{1,5},{5... | collective-permute-start | bytes 1916936 | tf_op jit(solution)/shard_map/ppermute | solution.py:91
  86.4 11.2 %collective-permute-start.11 = (bf16[256,768]{1,0:T(8,128)(2,1)S(1)}, bf16[256,768]{1,0:T(8,128)(2,1)S(1)}, u32[]{:S(2)}, u32[]{:S(2)}) collective-permute-start(bf16[256,768]{1,0:T(8,128)(2,1)S(1)} %get-tuple-element.153), channel_id=1, source_target_pairs={{0,4},{4,0},{8,12},{12,8},{16,20},{20,16},{24,28},{28,24},{1,5},{5... | collective-permute-start | bytes 1179656 | tf_op jit(solution)/shard_map/ppermute | solution.py:91
  87.9 11.0 %collective-permute-start.12 = (bf16[256,768]{1,0:T(8,128)(2,1)S(1)}, bf16[256,768]{1,0:T(8,128)(2,1)}, u32[]{:S(2)}, u32[]{:S(2)}) collective-permute-start(bf16[256,768]{1,0:T(8,128)(2,1)S(1)} %get-tuple-element.152), channel_id=1, source_target_pairs={{0,2},{1,3},{2,0},{3,1},{4,6},{5,7},{6,4},{7,5},{8,10},{9,11},{10,... | collective-permute-start | bytes 1179656 | tf_op jit(solution)/shard_map/ppermute | solution.py:91
  100.9 37.1 %collective-permute-start.14 = (bf16[2,256,768]{2,1,0:T(8,128)(2,1)}, bf16[2,256,768]{2,1,0:T(8,128)(2,1)}, u32[]{:S(2)}, u32[]{:S(2)}) collective-permute-start(bf16[2,256,768]{2,1,0:T(8,128)(2,1)} %pad_maximum_fusion.10), channel_id=1, source_target_pairs={{0,4},{4,0},{8,12},{12,8},{16,20},{20,16},{24,28},{28,24},{1,5},{5... | collective-permute-start | bytes 2359304 | tf_op jit(solution)/shard_map/ppermute | solution.py:91
  103.9 34.1 %collective-permute-start.13 = (bf16[2,256,768]{2,1,0:T(8,128)(2,1)}, bf16[2,256,768]{2,1,0:T(8,128)(2,1)}, u32[]{:S(2)}, u32[]{:S(2)}) collective-permute-start(bf16[2,256,768]{2,1,0:T(8,128)(2,1)} %pad_maximum_fusion.9), channel_id=1, source_target_pairs={{0,2},{1,3},{2,0},{3,1},{4,6},{5,7},{6,4},{7,5},{8,10},{9,11},{10,... | collective-permute-start | bytes 2359304 | tf_op jit(solution)/shard_map/ppermute | solution.py:91
  106.5 21.6 %collective-permute-start.16 = (bf16[256,768]{1,0:T(8,128)(2,1)S(1)}, bf16[256,768]{1,0:T(8,128)(2,1)}, u32[]{:S(2)}, u32[]{:S(2)}) collective-permute-start(bf16[256,768]{1,0:T(8,128)(2,1)S(1)} %get-tuple-element.145), channel_id=1, source_target_pairs={{0,4},{4,0},{8,12},{12,8},{16,20},{20,16},{24,28},{28,24},{1,5},{5... | collective-permute-start | bytes 1179656 | tf_op jit(solution)/shard_map/ppermute | solution.py:91
  107.6 23.7 %collective-permute-start.17 = (bf16[256,768]{1,0:T(8,128)(2,1)S(1)}, bf16[256,768]{1,0:T(8,128)(2,1)}, u32[]{:S(2)}, u32[]{:S(2)}) collective-permute-start(bf16[256,768]{1,0:T(8,128)(2,1)S(1)} %get-tuple-element.144), channel_id=1, source_target_pairs={{0,2},{1,3},{2,0},{3,1},{4,6},{5,7},{6,4},{7,5},{8,10},{9,11},{10,... | collective-permute-start | bytes 1179656 | tf_op jit(solution)/shard_map/ppermute | solution.py:91
  133.4 17.8 %collective-permute-start.19 = (bf16[2,256,768]{2,1,0:T(8,128)(2,1)}, bf16[2,256,768]{2,1,0:T(8,128)(2,1)S(1)}, u32[]{:S(2)}, u32[]{:S(2)}) collective-permute-start(bf16[2,256,768]{2,1,0:T(8,128)(2,1)} %pad_maximum_fusion.12), channel_id=1, source_target_pairs={{0,4},{4,0},{8,12},{12,8},{16,20},{20,16},{24,28},{28,24},{1,5},{5... | collective-permute-start | bytes 2359304 | tf_op jit(solution)/shard_map/ppermute | solution.py:91
  136.5 17.7 %collective-permute-start.18 = (bf16[2,256,768]{2,1,0:T(8,128)(2,1)}, bf16[2,256,768]{2,1,0:T(8,128)(2,1)S(1)}, u32[]{:S(2)}, u32[]{:S(2)}) collective-permute-start(bf16[2,256,768]{2,1,0:T(8,128)(2,1)} %pad_maximum_fusion.11), channel_id=1, source_target_pairs={{0,2},{1,3},{2,0},{3,1},{4,6},{5,7},{6,4},{7,5},{8,10},{9,11},{10,... | collective-permute-start | bytes 2359304 | tf_op jit(solution)/shard_map/ppermute | solution.py:91
  144.4 21.1 %collective-permute-start.15 = (bf16[2,4,128,768]{3,2,0,1:T(8,128)(2,1)}, bf16[2,4,128,768]{3,2,0,1:T(8,128)(2,1)}, u32[]{:S(2)}, u32[]{:S(2)}) collective-permute-start(bf16[2,4,128,768]{3,2,0,1:T(8,128)(2,1)} %fusion.42), channel_id=1, source_target_pairs={{0,1},{1,0},{2,3},{3,2},{4,5},{5,4},{6,7},{7,6},{8,9},{9,8},{10,11... | collective-permute-start | bytes 4718600 | tf_op jit(solution)/shard_map/ppermute | solution.py:91
  197.2 212.9 %reduce-scatter.5.cloned.1.call-start = ((), (), s32[]{:S(2)}) async-start(), calls=%async_computation.4 | async-start | bytes 5898240 | tf_op jit(solution)/shard_map/reduce_scatter | solution.py:618
  200.3 28.5 %collective-permute-start.21 = (bf16[512,768]{1,0:T(8,128)(2,1)}, bf16[512,768]{1,0:T(8,128)(2,1)S(1)}, u32[]{:S(2)}, u32[]{:S(2)}) collective-permute-start(bf16[512,768]{1,0:T(8,128)(2,1)} %slice.226), channel_id=1, source_target_pairs={{0,1},{1,0},{2,3},{3,2},{4,5},{5,4},{6,7},{7,6},{8,9},{9,8},{10,11... | collective-permute-start | bytes 2359304 | tf_op jit(solution)/shard_map/ppermute | solution.py:91
  201.8 27.0 %collective-permute-start.23 = (bf16[512,768]{1,0:T(8,128)(2,1)}, bf16[512,768]{1,0:T(8,128)(2,1)S(1)}, u32[]{:S(2)}, u32[]{:S(2)}) collective-permute-start(bf16[512,768]{1,0:T(8,128)(2,1)} %slice.228), channel_id=1, source_target_pairs={{0,1},{1,0},{2,3},{3,2},{4,5},{5,4},{6,7},{7,6},{8,9},{9,8},{10,11... | collective-permute-start | bytes 2359304 | tf_op jit(solution)/shard_map/ppermute | solution.py:91
  243.1 36.7 %collective-permute-start.26 = (bf16[2,256,1536]{2,1,0:T(8,128)(2,1)S(1)}, bf16[2,256,1536]{2,1,0:T(8,128)(2,1)S(1)}, u32[]{:S(2)}, u32[]{:S(2)}) collective-permute-start(bf16[2,256,1536]{2,1,0:T(8,128)(2,1)S(1)} %pad_maximum_fusion.6), channel_id=1, source_target_pairs={{0,4},{4,0},{8,12},{12,8},{16,20},{20,16},{24,28},{28,24},{1,5},{5... | collective-permute-start | bytes 4718600 | tf_op jit(solution)/shard_map/ppermute | solution.py:91
  244.0 36.3 %collective-permute-start.25 = (bf16[2,256,1536]{2,1,0:T(8,128)(2,1)S(1)}, bf16[2,256,1536]{2,1,0:T(8,128)(2,1)}, u32[]{:S(2)}, u32[]{:S(2)}) collective-permute-start(bf16[2,256,1536]{2,1,0:T(8,128)(2,1)S(1)} %stack.335), channel_id=1, source_target_pairs={{0,2},{1,3},{2,0},{3,1},{4,6},{5,7},{6,4},{7,5},{8,10},{9,11},{10,... | collective-permute-start | bytes 4718600 | tf_op jit(solution)/shard_map/ppermute | solution.py:91
  284.3 19.4 %collective-permute-start.27 = (bf16[1,256,1536]{2,1,0:T(8,128)(2,1)}, bf16[1,256,1536]{2,1,0:T(8,128)(2,1)}, u32[]{:S(2)}, u32[]{:S(2)}) collective-permute-start(bf16[1,256,1536]{2,1,0:T(8,128)(2,1)} %get-tuple-element.121), channel_id=1, source_target_pairs={{0,4},{4,0},{8,12},{12,8},{16,20},{20,16},{24,28},{28,24},{1,5},{5... | collective-permute-start | bytes 2359304 | tf_op jit(solution)/shard_map/ppermute | solution.py:91
  285.2 18.8 %collective-permute-start.28 = (bf16[1,256,1536]{2,1,0:T(8,128)(2,1)}, bf16[1,256,1536]{2,1,0:T(8,128)(2,1)}, u32[]{:S(2)}, u32[]{:S(2)}) collective-permute-start(bf16[1,256,1536]{2,1,0:T(8,128)(2,1)} %get-tuple-element.120), channel_id=1, source_target_pairs={{0,2},{1,3},{2,0},{3,1},{4,6},{5,7},{6,4},{7,5},{8,10},{9,11},{10,... | collective-permute-start | bytes 2359304 | tf_op jit(solution)/shard_map/ppermute | solution.py:91
  337.0 10.3 %collective-permute-start.29 = (bf16[4,2,2,24,2304]{4,3,2,1,0:T(8,128)(2,1)}, bf16[4,2,2,24,2304]{4,3,2,1,0:T(8,128)(2,1)}, u32[]{:S(2)}, u32[]{:S(2)}) collective-permute-start(bf16[4,2,2,24,2304]{4,3,2,1,0:T(8,128)(2,1)} %get-tuple-element.124), channel_id=1, source_target_pairs={{0,1},{1,0},{2,3},{3,2},{4,5},{5,4},{6,7},{7,6},{8,9},{9,8},{10,11... | collective-permute-start | bytes 5308424 | tf_op jit(solution)/shard_map/ppermute | solution.py:91
  345.8 14.7 %collective-permute-start.33 = (bf16[4,2,24,896]{3,2,1,0:T(8,128)(2,1)}, bf16[4,2,24,896]{3,2,1,0:T(8,128)(2,1)}, u32[]{:S(2)}, u32[]{:S(2)}) collective-permute-start(bf16[4,2,24,896]{3,2,1,0:T(8,128)(2,1)} %copy_bitcast_fusion.5), channel_id=1, source_target_pairs={{0,2},{1,3},{2,0},{3,1},{4,6},{5,7},{6,4},{7,5},{8,10},{9,11},{10,... | collective-permute-start | bytes 1032200 | tf_op jit(solution)/shard_map/ppermute | solution.py:91
  351.0 15.1 %collective-permute-start.31 = (bf16[4,2,24,1152]{3,2,1,0:T(8,128)(2,1)}, bf16[4,2,24,1152]{3,2,1,0:T(8,128)(2,1)}, u32[]{:S(2)}, u32[]{:S(2)}) collective-permute-start(bf16[4,2,24,1152]{3,2,1,0:T(8,128)(2,1)} %copy_bitcast_fusion.2), channel_id=1, source_target_pairs={{0,2},{1,3},{2,0},{3,1},{4,6},{5,7},{6,4},{7,5},{8,10},{9,11},{10,... | collective-permute-start | bytes 1327112 | tf_op jit(solution)/shard_map/ppermute | solution.py:91
  352.4 13.7 %collective-permute-start.30 = (bf16[4,2,24,1152]{3,2,1,0:T(8,128)(2,1)}, bf16[4,2,24,1152]{3,2,1,0:T(8,128)(2,1)}, u32[]{:S(2)}, u32[]{:S(2)}) collective-permute-start(bf16[4,2,24,1152]{3,2,1,0:T(8,128)(2,1)} %copy_bitcast_fusion.3), channel_id=1, source_target_pairs={{0,4},{4,0},{8,12},{12,8},{16,20},{20,16},{24,28},{28,24},{1,5},{5... | collective-permute-start | bytes 1327112 | tf_op jit(solution)/shard_map/ppermute | solution.py:91
  368.6 11.7 %collective-permute-start.39 = (bf16[4,24,896]{2,1,0:T(8,128)(2,1)}, bf16[4,24,896]{2,1,0:T(8,128)(2,1)S(1)}, u32[]{:S(2)}, u32[]{:S(2)}) collective-permute-start(bf16[4,24,896]{2,1,0:T(8,128)(2,1)} %dynamic-slice_bitcast_fusion.3), channel_id=1, source_target_pairs={{0,4},{4,0},{8,12},{12,8},{16,20},{20,16},{24,28},{28,24},{1,5},{5... | collective-permute-start | bytes 516104 | tf_op jit(solution)/shard_map/ppermute | solution.py:91
  386.3 20.5 %all-to-all-start = ((bf16[4,24,3200]{2,1,0:T(8,128)(2,1)}), bf16[4,24,3200]{2,1,0:T(8,128)(2,1)S(1)}, u32[]{:S(2)}, u32[]{:S(2)}) async-start(bf16[4,24,3200]{2,1,0:T(8,128)(2,1)} %pad_maximum_fusion.13), calls=%async_computation.1 | async-start | bytes 1228800 | tf_op jit(solution)/shard_map/all_to_all | solution.py:229
  (130 other events, 581.7 us)
Sparse Core Ops, SparseCore 0:
  22.8 88.9 all-gather.4
  113.4 87.8 all-gather.6
  203.6 83.6 reduce-scatter.2
  289.5 85.7 reduce-scatter.4
where the time goes:
time: 432 us; the launch traced here: 425 us
  waiting for transfers between devices  124 us (29%)
  Pallas kernels  88.9 us (21%)
  other arithmetic  59.8 us (14%)
  local copies, waits for them, and re-layouts  59.1 us (14%)
  starting transfers between devices  51.2 us (12%)
  matrix products  26.6 us (6%)
  between operations  15.4 us (4%)
    ppermute x38, waiting for transfers between devices, swap(): return lax.ppermute(value, axis, [(i, i ^ mask) for i in range(count)])  117 us
    pallas_call x2, Pallas kernels, run_expert(): pl.pallas_call(expert_kernel, grid=(chunks,), in_specs=[rows_in, rows_in,...  48.8 us
    ppermute x38, starting transfers between devices, swap(): return lax.ppermute(value, axis, [(i, i ^ mask) for i in range(count)])  35.7 us
    unnamed x237, local copies, waits for them, and re-layouts  19.9 us
    pallas_call x1, Pallas kernels, attend_back(): pl.pallas_call(attend_back_kernel, grid=(count,), in_specs=[column_from(b...  16.5 us
    pallas_call x1, Pallas kernels, attend_forward(): pl.pallas_call(attend_kernel, grid=(pairs,), in_specs=[pl.BlockSpec((slot...  15.4 us
    ppermute x6, starting transfers between devices, ring_shift(): lax.ppermute(value, 'fsdp', [(i, (i - 2 * by) % count) for i in range(cou...  11.1 us
    convert_element_type x8, other arithmetic, halve(): (a.astype(FULL) + b.astype(FULL)).astype(LOW)  10.6 us
  transfers between devices with their start and end apart: 49, of which 24 were waited for; matrix products, arithmetic and copies ran while one was open for 28% of the time, Pallas kernels for 21%

commit v1 on v0

--- a/solution.py
+++ b/solution.py
@@ -401,7 +401,7 @@
     chunk = pl.program_id(0)
     count, width = rows.shape[1:]
     units = weights.shape[2]
-    step = min(256, count)
+    step = min(512, count)
     second = second_of(weights)
 
     @pl.when(chunk == 0)

time: 432 us -> 432 us (level)
  no operation moved by 1% of the time
where the time goes in v1:
time: 432 us; the launch traced here: 426 us
  waiting for transfers between devices  126 us (29%)
  Pallas kernels  89.7 us (21%)
  other arithmetic  59.4 us (14%)
  local copies, waits for them, and re-layouts  59.1 us (14%)
  starting transfers between devices  49.8 us (12%)
  matrix products  26.8 us (6%)
  between operations  15.3 us (4%)
    ppermute x38, waiting for transfers between devices, swap(): return lax.ppermute(value, axis, [(i, i ^ mask) for i in range(count)])  119 us
    pallas_call x2, Pallas kernels, run_expert(): pl.pallas_call(expert_kernel, grid=(chunks,), in_specs=[rows_in, rows_in,...  49.7 us
    ppermute x38, starting transfers between devices, swap(): return lax.ppermute(value, axis, [(i, i ^ mask) for i in range(count)])  34.7 us
    unnamed x237, local copies, waits for them, and re-layouts  19.9 us
    pallas_call x1, Pallas kernels, attend_back(): pl.pallas_call(attend_back_kernel, grid=(count,), in_specs=[column_from(b...  16.4 us
    pallas_call x1, Pallas kernels, attend_forward(): pl.pallas_call(attend_kernel, grid=(pairs,), in_specs=[pl.BlockSpec((slot...  15.4 us
    ppermute x6, starting transfers between devices, ring_shift(): lax.ppermute(value, 'fsdp', [(i, (i - 2 * by) % count) for i in range(cou...  11.1 us
    convert_element_type x8, other arithmetic, halve(): (a.astype(FULL) + b.astype(FULL)).astype(LOW)  10.5 us
  transfers between devices with their start and end apart: 49, of which 24 were waited for; matrix products, arithmetic and copies ran while one was open for 28% of the time, Pallas kernels for 21%

profile of v1, /device:TPU:0, one launch (start us, length us, event | category | flops | bytes accessed | tf_op | source)
XLA Modules:
  0.0 425.9 jit_solution(2150778237475271282)
XLA Ops:
  9.8 5.1 %collective-permute-start = (bf16[24,3200]{1,0:T(8,128)(2,1)S(1)}, bf16[24,3200]{1,0:T(8,128)(2,1)S(1)}, u32[]{:S(2)}, u32[]{:S(2)}) collective-permute-start(bf16[24,3200]{1,0:T(8,128)(2,1)S(1)} %concatenate.159), channel_id=1, source_target_pairs={{0,24},{4,28},{8,0},{12,4},{16,8},{20,12},{24,16},{28,20},{1,25},{... | collective-permute-start | bytes 460808 | tf_op jit(solution)/shard_map/ppermute | solution.py:106
  24.1 2.2 pad_maximum_fusion.8.refs_0_
  45.2 4.0 collective-permute-done.3
  52.3 6.7 %collective-permute-done.7 = bf16[2,4,24,1536]{3,2,1,0:T(8,128)(2,1)S(1)} collective-permute-done((bf16[2,4,24,1536]{3,2,1,0:T(8,128)(2,1)S(1)}, bf16[2,4,24,1536]{3,2,1,0:T(8,128)(2,1)S(1)}, u32[]{:S(2)}, u32[]{:S(2)}) %collective-permute-start.7) | collective-permute-done | bytes 589856 | tf_op jit(solution)/shard_map/ppermute | solution.py:91
  65.3 3.5 convolution_convert_fusion.1.query.key.value
  68.9 15.4 %attend_forward.1 = (bf16[512,768]{1,0:T(8,128)(2,1)S(1)}, bf16[12,512,512]{2,1,0:T(8,128)(2,1)}) custom-call(bf16[512,2304]{1,0:T(8,128)(2,1)} %convolution_convert_fusion.1.query.key.value, bf16[512,2304]{1,0:T(8,128)(2,1)} %convolution_convert_fusion.1.query.key.value, bf16[512,2304]{1,0:T(8,128)(2,1)} %convolution_convert_fusion.1.query.key.value, ...), custom_call_target="tpu_custom_call" | custom-call | flops 50331648 | bytes 147456 | tf_op jit(solution)/shard_map/attend_forward/pallas_call | solution.py:281
  92.1 5.5 %collective-permute-done.11.refs_0_ = bf16[256,768]{1,0:T(8,128)(2,1)S(1)} collective-permute-done((bf16[256,768]{1,0:T(8,128)(2,1)S(1)}, bf16[256,768]{1,0:T(8,128)(2,1)S(1)}, u32[]{:S(2)}, u32[]{:S(2)}) %collective-permute-start.11) | collective-permute-done | bytes 393248 | tf_op jit(solution)/shard_map/ppermute | solution.py:91
  109.9 18.2 %collective-permute-done.16.refs_0_ = bf16[256,768]{1,0:T(8,128)(2,1)} collective-permute-done((bf16[256,768]{1,0:T(8,128)(2,1)S(1)}, bf16[256,768]{1,0:T(8,128)(2,1)}, u32[]{:S(2)}, u32[]{:S(2)}) %collective-permute-start.16) | collective-permute-done | bytes 393248 | tf_op jit(solution)/shard_map/ppermute | solution.py:91
  128.1 3.2 collective-permute-done.17.refs_1_
  142.1 2.4 fusion.42
  144.5 6.7 %collective-permute-done.19.refs_1_ = bf16[2,256,768]{2,1,0:T(8,128)(2,1)S(1)} collective-permute-done((bf16[2,256,768]{2,1,0:T(8,128)(2,1)}, bf16[2,256,768]{2,1,0:T(8,128)(2,1)S(1)}, u32[]{:S(2)}, u32[]{:S(2)}) %collective-permute-start.19) | collective-permute-done | bytes 786464 | tf_op jit(solution)/shard_map/ppermute | solution.py:91
  151.2 3.0 collective-permute-done.18.refs_0_
  158.3 2.5 fusion.39
  160.8 2.8 fusion.48
  173.1 24.8 %run_expert.2 = (bf16[1024,768]{1,0:T(8,128)(2,1)S(1)}, bf16[1024,768]{1,0:T(8,128)(2,1)}, bf16[4,1536,384]{2,1,0:T(8,128)(2,1)}) custom-call(bf16[2,1024,768]{2,1,0:T(8,128)(2,1)} %bitcast.233, bf16[2,1024,768]{2,1,0:T(8,128)(2,1)} %bitcast.235, bf16[4,1536,384]{2,1,0:T(8,128)(2,1)} %bitcast.244), custom_call_target="tpu_custom_call" | custom-call | flops 226492416 | bytes 245760 | tf_op jit(solution)/shard_map/run_expert/pallas_call | solution.py:444
  202.2 24.9 %run_expert.3 = (bf16[1024,768]{1,0:T(8,128)(2,1)S(1)}, bf16[1024,768]{1,0:T(8,128)(2,1)}, bf16[4,1536,384]{2,1,0:T(8,128)(2,1)}) custom-call(bf16[2,1024,768]{2,1,0:T(8,128)(2,1)} %bitcast.234, bf16[2,1024,768]{2,1,0:T(8,128)(2,1)} %bitcast.236, bf16[4,1536,384]{2,1,0:T(8,128)(2,1)} %after.22.weights), custom_call_target="tpu_custom_call" | custom-call | flops 226492416 | bytes 245760 | tf_op jit(solution)/shard_map/run_expert/pallas_call | solution.py:444
  232.4 8.1 %place_rows.1 = bf16[4,512,1536]{2,1,0:T(8,128)(2,1)} custom-call(bf16[4,512,512]{2,1,0:T(8,128)(2,1)} %compare_convert_fusion.refs_2_.hot, bf16[1024,768]{1,0:T(8,128)(2,1)} %copy-done.2, bf16[1024,768]{1,0:T(8,128)(2,1)} %copy-done.3, bf16[512,768]{1,0:T(8,128)(2,1)S(1)} %collective-permute-done.21.refs_2_, ...), custom_call_target="tpu_custom_call" | custom-call | flops 50331648 | bytes 196608 | tf_op jit(solution)/shard_map/place_rows/pallas_call | solution.py:481
  246.0 34.4 %collective-permute-done.26.refs_1_ = bf16[2,256,1536]{2,1,0:T(8,128)(2,1)S(1)} collective-permute-done((bf16[2,256,1536]{2,1,0:T(8,128)(2,1)S(1)}, bf16[2,256,1536]{2,1,0:T(8,128)(2,1)S(1)}, u32[]{:S(2)}, u32[]{:S(2)}) %collective-permute-start.26) | collective-permute-done | bytes 1572896 | tf_op jit(solution)/shard_map/ppermute | solution.py:91
  281.6 3.4 add_convert_fusion.1
  288.0 16.4 %collective-permute-done.27.refs_0_ = bf16[1,256,1536]{2,1,0:T(8,128)(2,1)} collective-permute-done((bf16[1,256,1536]{2,1,0:T(8,128)(2,1)}, bf16[1,256,1536]{2,1,0:T(8,128)(2,1)}, u32[]{:S(2)}, u32[]{:S(2)}) %collective-permute-start.27) | collective-permute-done | bytes 786464 | tf_op jit(solution)/shard_map/ppermute | solution.py:91
  305.0 2.9 add_bitcast_fusion.1
  315.9 16.4 %attend_back.1 = (bf16[512,768]{1,0:T(8,128)(2,1)S(1)}, bf16[512,768]{1,0:T(8,128)(2,1)S(1)}, bf16[512,768]{1,0:T(8,128)(2,1)}, f32[12,8,1024]{2,1,0:T(8,128)S(1)}) custom-call(bf16[512,2304]{1,0:T(8,128)(2,1)} %convolution_convert_fusion.1.query.key.value, bf16[512,2304]{1,0:T(8,128)(2,1)} %convolution_convert_fusion.1.query.key.value, ...), custom_call_target="tpu_custom_call" | custom-call | flops 100663296 | bytes 184320 | tf_op jit(solution)/shard_map/attend_back/pallas_call | solution.py:362
  333.8 2.1 convolution_convert_fusion
  335.9 2.1 dynamic-slice_bitcast_fusion
  348.4 2.6 fusion
  354.7 3.8 fusion.36
  361.4 5.8 %collective-permute-done.35.refs_4_ = f32[9,128]{1,0:T(8,128)S(1)} collective-permute-done((f32[9,128]{1,0:T(8,128)S(1)}, f32[9,128]{1,0:T(8,128)S(1)}, u32[]{:S(2)}, u32[]{:S(2)}) %collective-permute-start.35) | collective-permute-done | bytes 4640 | tf_op jit(solution)/shard_map/ppermute | solution.py:91
  378.2 3.2 collective-permute-done.40.refs_3_
  387.4 3.9 all-to-all-start
  392.5 3.1 fusion.30
  395.6 3.9 collective-permute-start.41
  400.8 6.6 %collective-permute-done.42.refs_2_ = f32[9,128]{1,0:T(8,128)S(1)} collective-permute-done((f32[9,128]{1,0:T(8,128)S(1)}, f32[9,128]{1,0:T(8,128)S(1)}, u32[]{:S(2)}, u32[]{:S(2)}) %collective-permute-start.42) | collective-permute-done | bytes 4640 | tf_op jit(solution)/shard_map/ppermute | solution.py:106
  (481 shorter events, 160.9 us)
Async XLA Ops:
  7.2 165.9 %all-gather.5.cloned.1.call-start = ((), (), s32[]{:S(2)}) async-start(), calls=%async_computation.5 | async-start | bytes 5898240 | tf_op jit(solution)/shard_map/all_gather | solution.py:552
  9.8 20.8 %collective-permute-start = (bf16[24,3200]{1,0:T(8,128)(2,1)S(1)}, bf16[24,3200]{1,0:T(8,128)(2,1)S(1)}, u32[]{:S(2)}, u32[]{:S(2)}) collective-permute-start(bf16[24,3200]{1,0:T(8,128)(2,1)S(1)} %concatenate.159), channel_id=1, source_target_pairs={{0,24},{4,28},{8,0},{12,4},{16,8},{20,12},{24,16},{28,20},{1,25},{... | collective-permute-start | bytes 460808 | tf_op jit(solution)/shard_map/ppermute | solution.py:106
  14.9 15.8 %collective-permute-start.1 = (bf16[24,3200]{1,0:T(8,128)(2,1)S(1)}, bf16[24,3200]{1,0:T(8,128)(2,1)}, u32[]{:S(2)}, u32[]{:S(2)}) collective-permute-start(bf16[24,3200]{1,0:T(8,128)(2,1)S(1)} %concatenate.159), channel_id=1, source_target_pairs={{0,16},{4,20},{8,24},{12,28},{16,0},{20,4},{24,8},{28,12},{1,17},{... | collective-permute-start | bytes 460808 | tf_op jit(solution)/shard_map/ppermute | solution.py:106
  14.9 16.7 %collective-permute-start.2 = (bf16[24,3200]{1,0:T(8,128)(2,1)S(1)}, bf16[24,3200]{1,0:T(8,128)(2,1)}, u32[]{:S(2)}, u32[]{:S(2)}) collective-permute-start(bf16[24,3200]{1,0:T(8,128)(2,1)S(1)} %concatenate.159), channel_id=1, source_target_pairs={{0,8},{4,12},{8,16},{12,20},{16,24},{20,28},{24,0},{28,4},{1,9},{5... | collective-permute-start | bytes 460808 | tf_op jit(solution)/shard_map/ppermute | solution.py:106
  17.7 8.7 %collective-permute-start.9 = (s32[1,512]{1,0:T(1,128)S(1)}, s32[1,512]{1,0:T(1,128)S(1)}, u32[]{:S(2)}, u32[]{:S(2)}) collective-permute-start(s32[1,512]{1,0:T(1,128)S(1)} %bitcast_add_fusion.1), channel_id=1, source_target_pairs={{0,4},{4,0},{8,12},{12,8},{16,20},{20,16},{24,28},{28,24},{1,5},{5... | collective-permute-start | bytes 6152 | tf_op jit(solution)/shard_map/ppermute | solution.py:91
  22.7 179.5 %all-gather.7.cloned.1.call-start = ((), (), s32[]{:S(2)}) async-start(), calls=%async_computation.6 | async-start | bytes 5898240 | tf_op jit(solution)/shard_map/all_gather | solution.py:552
  39.0 10.3 %collective-permute-start.3 = (bf16[4,24,1664]{2,1,0:T(8,128)(2,1)}, bf16[4,24,1664]{2,1,0:T(8,128)(2,1)S(1)}, u32[]{:S(2)}, u32[]{:S(2)}) collective-permute-start(bf16[4,24,1664]{2,1,0:T(8,128)(2,1)} %constant_dynamic-slice_fusion.1), channel_id=1, source_target_pairs={{0,2},{1,3},{2,0},{3,1},{4,6},{5,7},{6,4},{7,5},{8,10},{9,11},{10,... | collective-permute-start | bytes 958472 | tf_op jit(solution)/shard_map/ppermute | solution.py:91
  41.3 274.6 %reduce-scatter.3.cloned.1.call-start = ((), (), s32[]{:S(2)}) async-start(), calls=%async_computation.3 | async-start | bytes 5898240 | tf_op jit(solution)/shard_map/reduce_scatter | solution.py:618
  43.6 15.3 %collective-permute-start.7 = (bf16[2,4,24,1536]{3,2,1,0:T(8,128)(2,1)S(1)}, bf16[2,4,24,1536]{3,2,1,0:T(8,128)(2,1)S(1)}, u32[]{:S(2)}, u32[]{:S(2)}) collective-permute-start(bf16[2,4,24,1536]{3,2,1,0:T(8,128)(2,1)S(1)} %maximum_select_fusion.8), channel_id=1, source_target_pairs={{0,2},{1,3},{2,0},{3,1},{4,6},{5,7},{6,4},{7,5},{8,10},{9,11},{10,... | collective-permute-start | bytes 1769480 | tf_op jit(solution)/shard_map/ppermute | solution.py:91
  49.4 10.5 %collective-permute-start.4 = (bf16[2,4,24,1664]{3,2,1,0:T(8,128)(2,1)S(1)}, bf16[2,4,24,1664]{3,2,1,0:T(8,128)(2,1)S(1)}, u32[]{:S(2)}, u32[]{:S(2)}) collective-permute-start(bf16[2,4,24,1664]{3,2,1,0:T(8,128)(2,1)S(1)} %maximum_select_fusion.6), channel_id=1, source_target_pairs={{0,4},{4,0},{8,12},{12,8},{16,20},{20,16},{24,28},{28,24},{1,5},{5... | collective-permute-start | bytes 1916936 | tf_op jit(solution)/shard_map/ppermute | solution.py:91
  86.4 11.2 %collective-permute-start.11 = (bf16[256,768]{1,0:T(8,128)(2,1)S(1)}, bf16[256,768]{1,0:T(8,128)(2,1)S(1)}, u32[]{:S(2)}, u32[]{:S(2)}) collective-permute-start(bf16[256,768]{1,0:T(8,128)(2,1)S(1)} %get-tuple-element.153), channel_id=1, source_target_pairs={{0,4},{4,0},{8,12},{12,8},{16,20},{20,16},{24,28},{28,24},{1,5},{5... | collective-permute-start | bytes 1179656 | tf_op jit(solution)/shard_map/ppermute | solution.py:91
  87.9 11.0 %collective-permute-start.12 = (bf16[256,768]{1,0:T(8,128)(2,1)S(1)}, bf16[256,768]{1,0:T(8,128)(2,1)}, u32[]{:S(2)}, u32[]{:S(2)}) collective-permute-start(bf16[256,768]{1,0:T(8,128)(2,1)S(1)} %get-tuple-element.152), channel_id=1, source_target_pairs={{0,2},{1,3},{2,0},{3,1},{4,6},{5,7},{6,4},{7,5},{8,10},{9,11},{10,... | collective-permute-start | bytes 1179656 | tf_op jit(solution)/shard_map/ppermute | solution.py:91
  100.9 37.1 %collective-permute-start.14 = (bf16[2,256,768]{2,1,0:T(8,128)(2,1)}, bf16[2,256,768]{2,1,0:T(8,128)(2,1)}, u32[]{:S(2)}, u32[]{:S(2)}) collective-permute-start(bf16[2,256,768]{2,1,0:T(8,128)(2,1)} %pad_maximum_fusion.10), channel_id=1, source_target_pairs={{0,4},{4,0},{8,12},{12,8},{16,20},{20,16},{24,28},{28,24},{1,5},{5... | collective-permute-start | bytes 2359304 | tf_op jit(solution)/shard_map/ppermute | solution.py:91
  104.0 34.1 %collective-permute-start.13 = (bf16[2,256,768]{2,1,0:T(8,128)(2,1)}, bf16[2,256,768]{2,1,0:T(8,128)(2,1)}, u32[]{:S(2)}, u32[]{:S(2)}) collective-permute-start(bf16[2,256,768]{2,1,0:T(8,128)(2,1)} %pad_maximum_fusion.9), channel_id=1, source_target_pairs={{0,2},{1,3},{2,0},{3,1},{4,6},{5,7},{6,4},{7,5},{8,10},{9,11},{10,... | collective-permute-start | bytes 2359304 | tf_op jit(solution)/shard_map/ppermute | solution.py:91
  106.6 21.6 %collective-permute-start.16 = (bf16[256,768]{1,0:T(8,128)(2,1)S(1)}, bf16[256,768]{1,0:T(8,128)(2,1)}, u32[]{:S(2)}, u32[]{:S(2)}) collective-permute-start(bf16[256,768]{1,0:T(8,128)(2,1)S(1)} %get-tuple-element.145), channel_id=1, source_target_pairs={{0,4},{4,0},{8,12},{12,8},{16,20},{20,16},{24,28},{28,24},{1,5},{5... | collective-permute-start | bytes 1179656 | tf_op jit(solution)/shard_map/ppermute | solution.py:91
  107.6 23.7 %collective-permute-start.17 = (bf16[256,768]{1,0:T(8,128)(2,1)S(1)}, bf16[256,768]{1,0:T(8,128)(2,1)}, u32[]{:S(2)}, u32[]{:S(2)}) collective-permute-start(bf16[256,768]{1,0:T(8,128)(2,1)S(1)} %get-tuple-element.144), channel_id=1, source_target_pairs={{0,2},{1,3},{2,0},{3,1},{4,6},{5,7},{6,4},{7,5},{8,10},{9,11},{10,... | collective-permute-start | bytes 1179656 | tf_op jit(solution)/shard_map/ppermute | solution.py:91
  133.4 17.8 %collective-permute-start.19 = (bf16[2,256,768]{2,1,0:T(8,128)(2,1)}, bf16[2,256,768]{2,1,0:T(8,128)(2,1)S(1)}, u32[]{:S(2)}, u32[]{:S(2)}) collective-permute-start(bf16[2,256,768]{2,1,0:T(8,128)(2,1)} %pad_maximum_fusion.12), channel_id=1, source_target_pairs={{0,4},{4,0},{8,12},{12,8},{16,20},{20,16},{24,28},{28,24},{1,5},{5... | collective-permute-start | bytes 2359304 | tf_op jit(solution)/shard_map/ppermute | solution.py:91
  136.5 17.7 %collective-permute-start.18 = (bf16[2,256,768]{2,1,0:T(8,128)(2,1)}, bf16[2,256,768]{2,1,0:T(8,128)(2,1)S(1)}, u32[]{:S(2)}, u32[]{:S(2)}) collective-permute-start(bf16[2,256,768]{2,1,0:T(8,128)(2,1)} %pad_maximum_fusion.11), channel_id=1, source_target_pairs={{0,2},{1,3},{2,0},{3,1},{4,6},{5,7},{6,4},{7,5},{8,10},{9,11},{10,... | collective-permute-start | bytes 2359304 | tf_op jit(solution)/shard_map/ppermute | solution.py:91
  144.5 21.2 %collective-permute-start.15 = (bf16[2,4,128,768]{3,2,0,1:T(8,128)(2,1)}, bf16[2,4,128,768]{3,2,0,1:T(8,128)(2,1)}, u32[]{:S(2)}, u32[]{:S(2)}) collective-permute-start(bf16[2,4,128,768]{3,2,0,1:T(8,128)(2,1)} %fusion.42), channel_id=1, source_target_pairs={{0,1},{1,0},{2,3},{3,2},{4,5},{5,4},{6,7},{7,6},{8,9},{9,8},{10,11... | collective-permute-start | bytes 4718600 | tf_op jit(solution)/shard_map/ppermute | solution.py:91
  197.9 212.9 %reduce-scatter.5.cloned.1.call-start = ((), (), s32[]{:S(2)}) async-start(), calls=%async_computation.4 | async-start | bytes 5898240 | tf_op jit(solution)/shard_map/reduce_scatter | solution.py:618
  200.7 28.9 %collective-permute-start.21 = (bf16[512,768]{1,0:T(8,128)(2,1)}, bf16[512,768]{1,0:T(8,128)(2,1)S(1)}, u32[]{:S(2)}, u32[]{:S(2)}) collective-permute-start(bf16[512,768]{1,0:T(8,128)(2,1)} %slice.226), channel_id=1, source_target_pairs={{0,1},{1,0},{2,3},{3,2},{4,5},{5,4},{6,7},{7,6},{8,9},{9,8},{10,11... | collective-permute-start | bytes 2359304 | tf_op jit(solution)/shard_map/ppermute | solution.py:91
  202.1 27.5 %collective-permute-start.23 = (bf16[512,768]{1,0:T(8,128)(2,1)}, bf16[512,768]{1,0:T(8,128)(2,1)S(1)}, u32[]{:S(2)}, u32[]{:S(2)}) collective-permute-start(bf16[512,768]{1,0:T(8,128)(2,1)} %slice.228), channel_id=1, source_target_pairs={{0,1},{1,0},{2,3},{3,2},{4,5},{5,4},{6,7},{7,6},{8,9},{9,8},{10,11... | collective-permute-start | bytes 2359304 | tf_op jit(solution)/shard_map/ppermute | solution.py:91
  243.7 36.7 %collective-permute-start.26 = (bf16[2,256,1536]{2,1,0:T(8,128)(2,1)S(1)}, bf16[2,256,1536]{2,1,0:T(8,128)(2,1)S(1)}, u32[]{:S(2)}, u32[]{:S(2)}) collective-permute-start(bf16[2,256,1536]{2,1,0:T(8,128)(2,1)S(1)} %pad_maximum_fusion.6), channel_id=1, source_target_pairs={{0,4},{4,0},{8,12},{12,8},{16,20},{20,16},{24,28},{28,24},{1,5},{5... | collective-permute-start | bytes 4718600 | tf_op jit(solution)/shard_map/ppermute | solution.py:91
  244.5 36.6 %collective-permute-start.25 = (bf16[2,256,1536]{2,1,0:T(8,128)(2,1)S(1)}, bf16[2,256,1536]{2,1,0:T(8,128)(2,1)}, u32[]{:S(2)}, u32[]{:S(2)}) collective-permute-start(bf16[2,256,1536]{2,1,0:T(8,128)(2,1)S(1)} %stack.335), channel_id=1, source_target_pairs={{0,2},{1,3},{2,0},{3,1},{4,6},{5,7},{6,4},{7,5},{8,10},{9,11},{10,... | collective-permute-start | bytes 4718600 | tf_op jit(solution)/shard_map/ppermute | solution.py:91
  284.9 19.4 %collective-permute-start.27 = (bf16[1,256,1536]{2,1,0:T(8,128)(2,1)}, bf16[1,256,1536]{2,1,0:T(8,128)(2,1)}, u32[]{:S(2)}, u32[]{:S(2)}) collective-permute-start(bf16[1,256,1536]{2,1,0:T(8,128)(2,1)} %get-tuple-element.121), channel_id=1, source_target_pairs={{0,4},{4,0},{8,12},{12,8},{16,20},{20,16},{24,28},{28,24},{1,5},{5... | collective-permute-start | bytes 2359304 | tf_op jit(solution)/shard_map/ppermute | solution.py:91
  285.7 19.2 %collective-permute-start.28 = (bf16[1,256,1536]{2,1,0:T(8,128)(2,1)}, bf16[1,256,1536]{2,1,0:T(8,128)(2,1)}, u32[]{:S(2)}, u32[]{:S(2)}) collective-permute-start(bf16[1,256,1536]{2,1,0:T(8,128)(2,1)} %get-tuple-element.120), channel_id=1, source_target_pairs={{0,2},{1,3},{2,0},{3,1},{4,6},{5,7},{6,4},{7,5},{8,10},{9,11},{10,... | collective-permute-start | bytes 2359304 | tf_op jit(solution)/shard_map/ppermute | solution.py:91
  338.0 10.4 %collective-permute-start.29 = (bf16[4,2,2,24,2304]{4,3,2,1,0:T(8,128)(2,1)}, bf16[4,2,2,24,2304]{4,3,2,1,0:T(8,128)(2,1)}, u32[]{:S(2)}, u32[]{:S(2)}) collective-permute-start(bf16[4,2,2,24,2304]{4,3,2,1,0:T(8,128)(2,1)} %get-tuple-element.124), channel_id=1, source_target_pairs={{0,1},{1,0},{2,3},{3,2},{4,5},{5,4},{6,7},{7,6},{8,9},{9,8},{10,11... | collective-permute-start | bytes 5308424 | tf_op jit(solution)/shard_map/ppermute | solution.py:91
  346.9 14.1 %collective-permute-start.33 = (bf16[4,2,24,896]{3,2,1,0:T(8,128)(2,1)}, bf16[4,2,24,896]{3,2,1,0:T(8,128)(2,1)}, u32[]{:S(2)}, u32[]{:S(2)}) collective-permute-start(bf16[4,2,24,896]{3,2,1,0:T(8,128)(2,1)} %copy_bitcast_fusion.5), channel_id=1, source_target_pairs={{0,2},{1,3},{2,0},{3,1},{4,6},{5,7},{6,4},{7,5},{8,10},{9,11},{10,... | collective-permute-start | bytes 1032200 | tf_op jit(solution)/shard_map/ppermute | solution.py:91
  352.0 15.1 %collective-permute-start.31 = (bf16[4,2,24,1152]{3,2,1,0:T(8,128)(2,1)}, bf16[4,2,24,1152]{3,2,1,0:T(8,128)(2,1)}, u32[]{:S(2)}, u32[]{:S(2)}) collective-permute-start(bf16[4,2,24,1152]{3,2,1,0:T(8,128)(2,1)} %copy_bitcast_fusion.2), channel_id=1, source_target_pairs={{0,2},{1,3},{2,0},{3,1},{4,6},{5,7},{6,4},{7,5},{8,10},{9,11},{10,... | collective-permute-start | bytes 1327112 | tf_op jit(solution)/shard_map/ppermute | solution.py:91
  353.5 13.7 %collective-permute-start.30 = (bf16[4,2,24,1152]{3,2,1,0:T(8,128)(2,1)}, bf16[4,2,24,1152]{3,2,1,0:T(8,128)(2,1)}, u32[]{:S(2)}, u32[]{:S(2)}) collective-permute-start(bf16[4,2,24,1152]{3,2,1,0:T(8,128)(2,1)} %copy_bitcast_fusion.3), channel_id=1, source_target_pairs={{0,4},{4,0},{8,12},{12,8},{16,20},{20,16},{24,28},{28,24},{1,5},{5... | collective-permute-start | bytes 1327112 | tf_op jit(solution)/shard_map/ppermute | solution.py:91
  369.7 11.7 %collective-permute-start.39 = (bf16[4,24,896]{2,1,0:T(8,128)(2,1)}, bf16[4,24,896]{2,1,0:T(8,128)(2,1)S(1)}, u32[]{:S(2)}, u32[]{:S(2)}) collective-permute-start(bf16[4,24,896]{2,1,0:T(8,128)(2,1)} %dynamic-slice_bitcast_fusion.3), channel_id=1, source_target_pairs={{0,4},{4,0},{8,12},{12,8},{16,20},{20,16},{24,28},{28,24},{1,5},{5... | collective-permute-start | bytes 516104 | tf_op jit(solution)/shard_map/ppermute | solution.py:91
  387.4 20.0 %all-to-all-start = ((bf16[4,24,3200]{2,1,0:T(8,128)(2,1)}), bf16[4,24,3200]{2,1,0:T(8,128)(2,1)S(1)}, u32[]{:S(2)}, u32[]{:S(2)}) async-start(bf16[4,24,3200]{2,1,0:T(8,128)(2,1)} %pad_maximum_fusion.13), calls=%async_computation.1 | async-start | bytes 1228800 | tf_op jit(solution)/shard_map/all_to_all | solution.py:229
  (130 other events, 582.3 us)
Sparse Core Ops, SparseCore 0:
  22.8 88.9 all-gather.4
  113.4 87.8 all-gather.6
  203.6 83.6 reduce-scatter.2
  289.5 85.7 reduce-scatter.4
